TPU v7x, 32 devices: a whole 2x2x4 slice. The times are simulated.
32 devices in a mesh: dp: 8 (over z, y), mp: 4 (over x, core).
Axes of the slice: x: 2, y: 2, z: 4, core: 2. Of those that a mesh axis runs over, the one named last changes fastest.
Arguments:
- query_hidden: bfloat16 [256, 32, 768], P('dp', None, 'mp'), may hold values from -6 to 6
- query_proj: bfloat16 [768, 128], P('mp'), may hold values from -0.21875 to 0.21875
- passages: bfloat16 [512, 128, 128], P(('dp', 'mp')), may hold values from -6 to 6
- teacher: float32 [256, 4, 64], P('dp'), may hold values from -8 to 8
- neg_blocks: int32 [256, 4], P('dp'), may hold values from 0 to 7, all different within a row; in each aligned block of 32 rows (0 to 31, 32 to 63, ...) at most 16 rows name the same one
Outputs:
- kl_loss: float32 [256], P('dp')
Inputs may be any that keep to these rules, and one draw needn't show every extreme that they name: `neg_blocks`: each query names 4 different blocks. Among the 32 queries of one dp index no block is named more than 16 times, and some block is named exactly 16 times.
All inputs are finite; a program needn't handle non-finite values.
Results may differ from a plain program's by a relative error of at most 0.0003.
Values may be sent and summed in bfloat16 or wider, within the bound.
A program may use at most 64 MiB of HBM per device.

v0:
```python
import jax
import jax.numpy as jnp
from jax import lax
from jax.sharding import PartitionSpec as P

softness = 0.1


def unit_rows(values):
    return values * lax.rsqrt(jnp.sum(values * values, axis=-1, keepdims=True) + 1e-06)


def soft_scores(slot_rows, passage_vecs):
    slot_count = slot_rows.shape[0]
    block_size = 16
    padded_count = -(-slot_count // block_size) * block_size
    blocked = slot_rows.reshape(
        padded_count // block_size, block_size, slot_rows.shape[1], slot_rows.shape[2]
    )

    def block_scores(slot_block):
        sims = jnp.einsum(
            "sie,pje->sipj", slot_block, passage_vecs, preferred_element_type=jnp.float32
        )
        softened = softness * jnp.log(jnp.sum(jnp.exp(sims / softness), axis=-1))
        return jnp.sum(softened, axis=1)

    scored = lax.map(block_scores, blocked)
    return scored.reshape(padded_count, -1)


def per_device(query_hidden, query_proj, passages, teacher, neg_blocks):
    partial_sum = jnp.einsum(
        "qth,he->qte", query_hidden, query_proj, preferred_element_type=jnp.float32
    )
    passage_vecs = unit_rows(passages.astype(jnp.float32)).astype(jnp.bfloat16)
    dp_count = lax.axis_size("dp")
    query_count, pick_count = neg_blocks.shape
    embed_width = partial_sum.shape[2]
    row_count = query_count * pick_count
    capacity = max(2, -(-row_count // dp_count))
    slots_all = dp_count * capacity
    owners = neg_blocks.reshape(row_count)
    owner_hits = (owners[:, None] == jnp.arange(dp_count, dtype=jnp.int32)[None, :]).astype(
        jnp.int32
    )
    earlier = jnp.cumsum(owner_hits, axis=0) - owner_hits
    slot_rank = jnp.sum(earlier * owner_hits, axis=1)
    slot_ids = owners * capacity + slot_rank
    matches = (slot_ids[None, :] == jnp.arange(slots_all, dtype=jnp.int32)[:, None]).astype(
        jnp.int32
    )
    row_query = jnp.arange(row_count, dtype=jnp.int32) // pick_count
    source = jnp.sum(matches * row_query[None, :], axis=1)
    filled = jnp.sum(matches, axis=1)
    token_share = lax.psum_scatter(partial_sum, "mp", scatter_dimension=1, tiled=True)
    share_vecs = unit_rows(token_share).astype(jnp.bfloat16)
    quarter = share_vecs.shape[1]
    token_part = share_vecs[source] * filled[:, None, None].astype(jnp.bfloat16)
    token_part = token_part.reshape(dp_count, capacity, quarter, embed_width)
    arrived = lax.all_to_all(token_part, "dp", split_axis=0, concat_axis=0, tiled=True)
    joined = lax.all_gather(arrived, "mp", axis=2, tiled=True)
    tokens = joined.shape[2]
    scores = soft_scores(joined.reshape(slots_all, tokens, embed_width), passage_vecs).reshape(
        dp_count, capacity, -1
    )
    returned = lax.all_to_all(scores, "dp", split_axis=0, concat_axis=0, tiled=True)
    home_scores = returned.reshape(slots_all, -1)[slot_ids].reshape(query_count, pick_count, -1)
    teacher_logp = teacher - jnp.log(jnp.sum(jnp.exp(teacher), axis=(1, 2), keepdims=True))
    student = lax.all_gather(home_scores, "mp", axis=2, tiled=True)
    kl_loss = jnp.sum(jnp.exp(teacher_logp) * (teacher_logp - student), axis=(1, 2)) + jnp.log(
        jnp.sum(jnp.exp(student), axis=(1, 2))
    )
    return kl_loss


def solution(mesh):
    in_specs = (
        P("dp", None, "mp"),
        P("mp", None),
        P(("dp", "mp"), None, None),
        P("dp", None, None),
        P("dp", None),
    )
    out_specs = P("dp")
    return jax.shard_map(
        per_device, mesh=mesh, in_specs=in_specs, out_specs=out_specs, check_vma=False
    )
```

profile of v0, /device:TPU:0, one launch (start us, length us, event | category | flops | bytes accessed | tf_op | source)
XLA Modules:
  0.0 113.8 jit_solution(1627998460622452568)
XLA Ops:
  6.5 0.0 copy-start
  6.5 0.0 copy-start.3
  6.5 0.0 reduce-scatter.2.cloned.1.call-start
  6.5 1.0 copy-done
  7.6 1.9 %fusion.7 = f32[32,32,128]{2,1,0:T(8,128)} fusion(bf16[32,32,192]{2,1,0:T(8,128)(2,1)S(1)} %copy-done, bf16[192,128]{1,0:T(8,128)(2,1)} %param.8), kind=kOutput, calls=%fused_computation.26 | convolution fusion | flops 50331648 | bytes 966656 | tf_op jit(solution)/shard_map/qth,he->qte/dot_general | solution.py:33
  9.5 0.0 reduce-scatter.2.cloned.1.call-update
  9.5 0.0 all-gather.2.cloned.1.call-start
  9.5 0.0 copy-done.3
  9.5 0.1 copy.19
  9.6 0.1 reshape.98
  9.7 0.1 fusion.6
  9.8 0.2 reduce_window_sum.11
  10.0 0.2 select_reduce_fusion.1
  10.2 0.1 convert_reduce_fusion
  10.3 0.1 convert_element_type.30
  10.4 23.8 %reduce-scatter.2.cloned.1.call-done = f32[32,8,128]{2,1,0:T(8,128)} async-done(((f32[32,32,128]{2,1,0:T(8,128)}), f32[32,8,128]{2,1,0:T(8,128)}) %reduce-scatter.2.cloned.1.call-update) | async-done | bytes 131088 | tf_op jit(solution)/shard_map/reduce_scatter | solution.py:56
  34.2 1.0 multiply_reduce_fusion.1
  35.3 0.0 copy-start.2
  35.3 0.0 copy-start.1
  35.3 1.1 multiply_convert_fusion
  36.4 0.7 gather_fusion
  37.1 0.2 broadcast_multiply_fusion
  37.3 14.3 %all_to_all.10 = bf16[8,16,8,128]{3,2,1,0:T(8,128)(2,1)} all-to-all(bf16[8,16,8,128]{3,2,1,0:T(8,128)(2,1)S(1)} %broadcast_multiply_fusion), channel_id=1, replica_groups=mesh['dp'=8,'mp'=4] {'dp'}, dimensions={0} | all-to-all | bytes 524288 | tf_op jit(solution)/shard_map/all_to_all | solution.py:61
  51.6 0.0 all-gather.2.cloned.1.call-update
  51.6 0.1 copy.20
  51.7 0.1 mul.87
  51.8 0.0 copy-done.2
  51.9 0.3 exponential_reduce_fusion.2
  52.2 0.0 copy-done.1
  52.2 0.3 fusion.4
  52.6 0.3 fusion.5
  52.9 13.8 %all-gather.2.cloned.1.call-done = bf16[8,16,32,128]{3,2,1,0:T(8,128)(2,1)} async-done(((bf16[8,16,8,128]{3,2,1,0:T(8,128)(2,1)}), bf16[8,16,32,128]{3,2,1,0:T(8,128)(2,1)}) %all-gather.2.cloned.1.call-update) | async-done | bytes 1048592 | tf_op jit(solution)/shard_map/all_gather | solution.py:62
  66.7 19.2 %while.10 = (s32[]{:T(128)}, f32[8,16,16]{2,1,0:T(8,128)S(1)}, bf16[8,16,32,128]{3,2,1,0:T(8,128)(2,1)}, bf16[16,128,128]{2,1,0:T(8,128)(2,1)S(1)}, s32[]{:T(128)}) while((s32[]{:T(128)}, f32[8,16,16]{2,1,0:T(8,128)S(1)}, bf16[8,16,32,128]{3,2,1,0:T(8,128)(2,1)}, bf16[16,128,128]{2,1,0:T(8,128)(2,1)S(1)}, s32[]{:T(128)}) %tuple.20), condition=%wide.region_11.12_spmd, body=%wide.region_8.11_spmd.sunk | while | flops 270540544 | bytes 738881 | solution.py:28
  66.7 2.2 %exponential_reduce_fusion.4 = f32[16,32,16]{1,2,0:T(8,128)S(1)} fusion(bf16[16,128,128]{2,1,0:T(8,128)(2,1)S(1)} %get-tuple-element.78, bf16[8,16,32,128]{3,2,1,0:T(8,128)(2,1)} %get-tuple-element.77, s32[]{:T(128)} %get-tuple-element.70), kind=kOutput, calls=%fused_computation.2.clone.1 | convolution fusion | flops 270524416 | bytes 688640 | tf_op jit(solution)/shard_map/while/body/eval_jaxpr/sie,pje->sipj/dot_general | solution.py:22
  69.0 0.1 multiply_reduce_fusion.4
  69.1 2.2 %exponential_reduce_fusion.4 = f32[16,32,16]{1,2,0:T(8,128)S(1)} fusion(bf16[16,128,128]{2,1,0:T(8,128)(2,1)S(1)} %get-tuple-element.78, bf16[8,16,32,128]{3,2,1,0:T(8,128)(2,1)} %get-tuple-element.77, s32[]{:T(128)} %get-tuple-element.70), kind=kOutput, calls=%fused_computation.2.clone.1 | convolution fusion | flops 270524416 | bytes 688640 | tf_op jit(solution)/shard_map/while/body/eval_jaxpr/sie,pje->sipj/dot_general | solution.py:22
  71.4 0.1 multiply_reduce_fusion.4
  71.5 2.2 %exponential_reduce_fusion.4 = f32[16,32,16]{1,2,0:T(8,128)S(1)} fusion(bf16[16,128,128]{2,1,0:T(8,128)(2,1)S(1)} %get-tuple-element.78, bf16[8,16,32,128]{3,2,1,0:T(8,128)(2,1)} %get-tuple-element.77, s32[]{:T(128)} %get-tuple-element.70), kind=kOutput, calls=%fused_computation.2.clone.1 | convolution fusion | flops 270524416 | bytes 688640 | tf_op jit(solution)/shard_map/while/body/eval_jaxpr/sie,pje->sipj/dot_general | solution.py:22
  73.8 0.1 multiply_reduce_fusion.4
  73.9 2.2 %exponential_reduce_fusion.4 = f32[16,32,16]{1,2,0:T(8,128)S(1)} fusion(bf16[16,128,128]{2,1,0:T(8,128)(2,1)S(1)} %get-tuple-element.78, bf16[8,16,32,128]{3,2,1,0:T(8,128)(2,1)} %get-tuple-element.77, s32[]{:T(128)} %get-tuple-element.70), kind=kOutput, calls=%fused_computation.2.clone.1 | convolution fusion | flops 270524416 | bytes 688640 | tf_op jit(solution)/shard_map/while/body/eval_jaxpr/sie,pje->sipj/dot_general | solution.py:22
  76.2 0.1 multiply_reduce_fusion.4
  76.3 2.2 %exponential_reduce_fusion.4 = f32[16,32,16]{1,2,0:T(8,128)S(1)} fusion(bf16[16,128,128]{2,1,0:T(8,128)(2,1)S(1)} %get-tuple-element.78, bf16[8,16,32,128]{3,2,1,0:T(8,128)(2,1)} %get-tuple-element.77, s32[]{:T(128)} %get-tuple-element.70), kind=kOutput, calls=%fused_computation.2.clone.1 | convolution fusion | flops 270524416 | bytes 688640 | tf_op jit(solution)/shard_map/while/body/eval_jaxpr/sie,pje->sipj/dot_general | solution.py:22
  78.6 0.1 multiply_reduce_fusion.4
  78.7 2.2 %exponential_reduce_fusion.4 = f32[16,32,16]{1,2,0:T(8,128)S(1)} fusion(bf16[16,128,128]{2,1,0:T(8,128)(2,1)S(1)} %get-tuple-element.78, bf16[8,16,32,128]{3,2,1,0:T(8,128)(2,1)} %get-tuple-element.77, s32[]{:T(128)} %get-tuple-element.70), kind=kOutput, calls=%fused_computation.2.clone.1 | convolution fusion | flops 270524416 | bytes 688640 | tf_op jit(solution)/shard_map/while/body/eval_jaxpr/sie,pje->sipj/dot_general | solution.py:22
  81.0 0.1 multiply_reduce_fusion.4
  81.1 2.2 %exponential_reduce_fusion.4 = f32[16,32,16]{1,2,0:T(8,128)S(1)} fusion(bf16[16,128,128]{2,1,0:T(8,128)(2,1)S(1)} %get-tuple-element.78, bf16[8,16,32,128]{3,2,1,0:T(8,128)(2,1)} %get-tuple-element.77, s32[]{:T(128)} %get-tuple-element.70), kind=kOutput, calls=%fused_computation.2.clone.1 | convolution fusion | flops 270524416 | bytes 688640 | tf_op jit(solution)/shard_map/while/body/eval_jaxpr/sie,pje->sipj/dot_general | solution.py:22
  83.4 0.1 multiply_reduce_fusion.4
  83.5 2.2 %exponential_reduce_fusion.4 = f32[16,32,16]{1,2,0:T(8,128)S(1)} fusion(bf16[16,128,128]{2,1,0:T(8,128)(2,1)S(1)} %get-tuple-element.78, bf16[8,16,32,128]{3,2,1,0:T(8,128)(2,1)} %get-tuple-element.77, s32[]{:T(128)} %get-tuple-element.70), kind=kOutput, calls=%fused_computation.2.clone.1 | convolution fusion | flops 270524416 | bytes 688640 | tf_op jit(solution)/shard_map/while/body/eval_jaxpr/sie,pje->sipj/dot_general | solution.py:22
  85.8 0.1 multiply_reduce_fusion.4
  85.9 0.7 reshape.120
  86.6 5.5 %all-to-all-start.1 = ((f32[8,1,256]{2,1,0:T(1,128)}), f32[8,1,256]{2,1,0:T(1,128)S(1)}, u32[]{:S(2)}, u32[]{:S(2)}) async-start(f32[8,1,256]{2,1,0:T(1,128)} %reshape.120), calls=%async_computation.2 | async-start | bytes 16384 | tf_op jit(solution)/shard_map/all_to_all | solution.py:67
  92.2 6.5 %all-to-all-done.1 = f32[8,1,256]{2,1,0:T(1,128)S(1)} async-done(((f32[8,1,256]{2,1,0:T(1,128)}), f32[8,1,256]{2,1,0:T(1,128)S(1)}, u32[]{:S(2)}, u32[]{:S(2)}) %all-to-all-start.1) | async-done | bytes 8224 | tf_op jit(solution)/shard_map/all_to_all | solution.py:67
  98.7 0.5 broadcast.110
  99.2 0.7 reduce
  99.8 0.1 reshape.121
  99.9 0.6 gather_fusion.1
  100.6 0.1 copy.21
  100.7 5.4 %all_gather.7 = f32[32,4,64]{0,1,2:T(4,128)S(1)} all-gather(f32[32,4,16]{0,1,2:T(4,128)S(1)} %copy.21), channel_id=1, replica_groups=mesh['dp'=8,'mp'=4] {'mp'}, dimensions={2}, use_global_device_ids=true | all-gather | bytes 40960 | tf_op jit(solution)/shard_map/all_gather | solution.py:70
  106.1 0.1 copy.22
  106.2 0.1 exponential_reduce_fusion.1
  106.3 0.2 multiply_reduce_fusion.2
  106.5 0.5 log_add_fusion
  (19 shorter events, 0.1 us)
Async XLA Ops:
  6.5 1.0 copy-start
  6.5 3.0 %copy-start.3 = (s32[32,4]{0,1:T(4,128)S(1)}, s32[32,4]{0,1:T(4,128)}, u32[]{:S(2)}) copy-start(s32[32,4]{0,1:T(4,128)} %param.11) | copy-start | bytes 1540
  6.5 27.7 %reduce-scatter.2.cloned.1.call-start = ((), (), s32[]{:S(2)}) async-start(), calls=%async_computation.3 | async-start | bytes 655360 | tf_op jit(solution)/shard_map/reduce_scatter | solution.py:56
  9.5 57.2 %all-gather.2.cloned.1.call-start = ((), (), s32[]{:S(2)}) async-start(), calls=%async_computation.4 | async-start | bytes 1310720 | tf_op jit(solution)/shard_map/all_gather | solution.py:62
  35.3 16.6 %copy-start.2 = (f32[32,4,64]{2,1,0:T(4,128)S(1)}, f32[32,4,64]{2,1,0:T(4,128)}, u32[]{:S(2)}) copy-start(f32[32,4,64]{2,1,0:T(4,128)} %param.10) | copy-start | bytes 98308
  35.3 16.9 %copy-start.1 = (bf16[16,128,128]{2,1,0:T(8,128)(2,1)S(1)}, bf16[16,128,128]{2,1,0:T(8,128)(2,1)}, u32[]{:S(2)}) copy-start(bf16[16,128,128]{2,1,0:T(8,128)(2,1)} %param.9) | copy-start | bytes 1572868
  86.6 12.0 %all-to-all-start.1 = ((f32[8,1,256]{2,1,0:T(1,128)}), f32[8,1,256]{2,1,0:T(1,128)S(1)}, u32[]{:S(2)}, u32[]{:S(2)}) async-start(f32[8,1,256]{2,1,0:T(1,128)} %reshape.120), calls=%async_computation.2 | async-start | bytes 16384 | tf_op jit(solution)/shard_map/all_to_all | solution.py:67
Sparse Core Ops, SparseCore 0:
  9.8 24.3 reduce-scatter.1
  51.7 14.9 all-gather.1
where the time goes:
time: 114 us
  waiting for transfers between devices  44.1 us (39%)
  matrix products  19.8 us (17%)
  blocking collectives  19.8 us (17%)
  between operations  13.6 us (12%)
  other arithmetic  6.29 us (6%)
  starting transfers between devices  5.56 us (5%)
  local copies, waits for them, and re-layouts  4.37 us (4%)
    reduce_scatter x1, waiting for transfers between devices, per_device(): lax.psum_scatter(partial_sum, 'mp', scatter_dimension=1, tiled=True)  23.8 us
    dot_general x8, matrix products, block_scores(): jnp.einsum('sie,pje->sipj', slot_block, passage_vecs, preferred_element_t...  18 us
    all_to_all x1, blocking collectives, per_device(): lax.all_to_all(token_part, 'dp', split_axis=0, concat_axis=0, tiled=True)  14.3 us
    all_gather x1, waiting for transfers between devices, per_device(): joined = lax.all_gather(arrived, 'mp', axis=2, tiled=True)  13.8 us
    all_to_all x1, waiting for transfers between devices, per_device(): lax.all_to_all(scores, 'dp', split_axis=0, concat_axis=0, tiled=True)  6.5 us
    all_to_all x1, starting transfers between devices, per_device(): lax.all_to_all(scores, 'dp', split_axis=0, concat_axis=0, tiled=True)  5.52 us
    all_gather x1, blocking collectives, per_device(): student = lax.all_gather(home_scores, 'mp', axis=2, tiled=True)  5.42 us
  transfers between devices with their start and end apart: 3, of which 3 were waited for; matrix products, arithmetic and copies ran while one was open for 2% of the time, Pallas kernels for 0%

commit v1 on v0

--- a/solution.py
+++ b/solution.py
@@ -1,13 +1,256 @@
+import functools
 import jax
 import jax.numpy as jnp
 from jax import lax
+from jax.experimental import pallas as pl
+from jax.experimental.pallas import tpu as pltpu
 from jax.sharding import PartitionSpec as P
 
 softness = 0.1
+log2_e = 1.4426950408889634
+group = 8
 
 
 def unit_rows(values):
     return values * lax.rsqrt(jnp.sum(values * values, axis=-1, keepdims=True) + 1e-06)
+
+
+def fused_kernel(
+    dp, mp, cap,
+    hid_ref, proj_ref, pas_ref, teach_ref, slotq_ref, slote_ref,
+    out_ref,
+    part, send_a, recv_a, pvecs, pick, send_b, queries, sums, send_r, recv_r, lp_perm,
+    a_send, a_recv, p_send, p_recv, b_send, b_recv, c_send, c_recv, r_send, r_recv,
+):
+    d = lax.axis_index("dp")
+    m = lax.axis_index("mp")
+    x, c = m // 2, m % 2
+    qd, qt = hid_ref.shape[0], hid_ref.shape[1]
+    emb = proj_ref.shape[1]
+    pick_count = teach_ref.shape[1]
+    share = qt // mp
+    half = cap // 2
+    rows_b = half * share
+    own_p = pas_ref.shape[0]
+    pt = pas_ref.shape[1]
+    chip_p = 2 * own_p
+    slots = dp * cap
+
+    def remote(src, dst, ssem, rsem, dd, mm):
+        return pltpu.make_async_remote_copy(
+            src_ref=src, dst_ref=dst, send_sem=ssem, recv_sem=rsem,
+            device_id=(dd, mm), device_id_type=pl.DeviceIdType.MESH,
+        )
+
+    barrier = pltpu.get_barrier_semaphore()
+    for j in range(dp):
+        for i in range(mp):
+            if j or i:
+                pl.semaphore_signal(
+                    barrier, inc=1, device_id=((d + j) % dp, (m + i) % mp),
+                    device_id_type=pl.DeviceIdType.MESH,
+                )
+
+    projected = jnp.dot(
+        hid_ref[...].reshape(qd * qt, hid_ref.shape[2]), proj_ref[...],
+        preferred_element_type=jnp.float32,
+    ).reshape(qd, qt, emb)
+    for k in range(mp):
+        piece = projected[:, k * share:(k + 1) * share, :].reshape(qd * share, emb)
+        part[k] = piece
+        send_a[k] = piece.astype(jnp.bfloat16)
+
+    pl.semaphore_wait(barrier, dp * mp - 1)
+
+    copies = []
+    for i in range(1, mp):
+        to = (m + i) % mp
+        cp = remote(send_a.at[to], recv_a.at[m], a_send.at[i], a_recv.at[m], d, to)
+        cp.start()
+        copies.append(cp)
+
+    pvecs[c] = unit_rows(pas_ref[...].reshape(own_p * pt, emb).astype(jnp.float32)).astype(
+        jnp.bfloat16
+    )
+    cp = remote(pvecs.at[c], pvecs.at[c], p_send, p_recv, d, 2 * x + 1 - c)
+    cp.start()
+    copies.append(cp)
+
+    row = lax.broadcasted_iota(jnp.int32, (cap * share, qd * share), 0)
+    for b in range(dp):
+        hit = slote_ref[0:1, :] == row + b * cap * share
+        for k in range(1, pick_count):
+            hit = hit | (slote_ref[k:k + 1, :] == row + b * cap * share)
+        pick[b] = jnp.where(hit, 1.0, 0.0).astype(jnp.bfloat16)
+
+    total = part[m]
+    for i in range(1, mp):
+        src = (m + i) % mp
+        remote(send_a.at[src], recv_a.at[src], a_send.at[i], a_recv.at[src], d, src).wait_recv()
+        total = total + recv_a[src].astype(jnp.float32)
+    share_vecs = unit_rows(total).astype(jnp.bfloat16)
+
+    for j in range(dp):
+        b = (d + j) % dp
+        chosen = jnp.dot(pick[b], share_vecs, preferred_element_type=jnp.float32).astype(
+            jnp.bfloat16
+        )
+        send_b[j] = chosen.reshape(2, rows_b, emb)
+        for cc in (1, 0):
+            to_c = c if cc == 0 else 1 - c
+            if j == 0 and cc == 0:
+                queries[d, m] = send_b[0, c]
+                continue
+            cp = remote(
+                send_b.at[j, to_c], queries.at[d, m], b_send.at[j, cc], b_recv.at[d, c],
+                b, 2 * x + to_c,
+            )
+            cp.start()
+            copies.append(cp)
+
+    slot_row = lax.broadcasted_iota(jnp.int32, (slots, qd), 0)
+    norm = jnp.zeros((qd, 1), jnp.float32)
+    for k in range(pick_count):
+        norm = norm + jnp.sum(jnp.exp(teach_ref[:, k, :]), axis=-1, keepdims=True)
+    log_norm = jnp.log(norm)
+    perm = jnp.zeros((slots, teach_ref.shape[2]), jnp.float32)
+    for k in range(pick_count):
+        place = jnp.where(slotq_ref[k:k + 1, :] == slot_row, 1.0, 0.0)
+        perm = perm + jnp.dot(
+            place, teach_ref[:, k, :] - log_norm, precision=lax.Precision.HIGHEST,
+            preferred_element_type=jnp.float32,
+        )
+    lp_perm[...] = perm
+
+    lane = lax.broadcasted_iota(jnp.int32, (half, mp * rows_b), 1)
+    slot_of = lax.broadcasted_iota(jnp.int32, (half, mp * rows_b), 0)
+    fold = jnp.where((lane // share) % half == slot_of, 1.0, 0.0)
+
+    def arrive(j):
+        src_d = (d - j + dp) % dp
+        for cc in (1, 0):
+            if j == 0 and cc == 0:
+                continue
+            src_c = c if cc == 0 else 1 - c
+            remote(
+                send_b.at[j, 0], queries.at[src_d, 2 * x + src_c], b_send.at[j, cc],
+                b_recv.at[src_d, src_c], src_d, 2 * x + src_c,
+            ).wait_recv()
+        mine = queries.at[src_d, pl.ds(2 * x, 2)]
+        fwd = remote(mine, mine, c_send.at[j], c_recv.at[src_d], d, 2 * (1 - x) + c)
+        fwd.start()
+        copies.append(fwd)
+
+    arrive(0)
+    remote(pvecs.at[1 - c], pvecs.at[1 - c], p_send, p_recv, d, 2 * x + 1 - c).wait_recv()
+    for j in range(dp):
+        if j + 1 < dp:
+            arrive(j + 1)
+        src_d = (d - j + dp) % dp
+        other = queries.at[src_d, pl.ds(2 * (1 - x), 2)]
+        remote(other, other, c_send.at[j], c_recv.at[src_d], d, 2 * (1 - x) + c).wait_recv()
+        tokens = queries[src_d].reshape(mp * rows_b, emb)
+
+        def score(g, carry):
+            at = g * group
+            passages = pvecs[at // own_p, pl.ds(pl.multiple_of((at % own_p) * pt, pt), group * pt), :]
+            sims = lax.dot_general(
+                passages, tokens, (((1,), (1,)), ((), ())), preferred_element_type=jnp.float32
+            )
+            weights = jnp.exp2(sims * (log2_e / softness)).reshape(group, pt, mp * rows_b)
+            sums[pl.ds(pl.multiple_of(at, group), group), :] = jnp.sum(weights, axis=1)
+            return carry
+
+        lax.fori_loop(0, chip_p // group, score, 0)
+        soft = softness * jnp.log(sums[...])
+        student = lax.dot_general(
+            fold, soft, (((1,), (1,)), ((), ())), precision=lax.Precision.HIGHEST,
+            preferred_element_type=jnp.float32,
+        )
+        send_r[j, :, 0:chip_p] = student
+        for i in range(mp):
+            to = (m + i) % mp
+            if j == 0 and i == 0:
+                recv_r[d, m, :, 0:chip_p] = student
+                continue
+            cp = remote(
+                send_r.at[j], recv_r.at[d, m], r_send.at[j, i], r_recv.at[d, m], src_d, to
+            )
+            cp.start()
+            copies.append(cp)
+
+    for j in range(dp):
+        b = (d + j) % dp
+        for i in range(mp):
+            if j or i:
+                src = (m + i) % mp
+                remote(
+                    send_r.at[j], recv_r.at[b, src], r_send.at[j, i], r_recv.at[b, src], b, src
+                ).wait_recv()
+
+    place = jnp.zeros((slots, qd), jnp.float32)
+    for k in range(pick_count):
+        place = place + jnp.where(slotq_ref[k:k + 1, :] == slot_row, 1.0, 0.0)
+    cross = jnp.zeros((slots, 1), jnp.float32)
+    mass = jnp.zeros((slots, 1), jnp.float32)
+    for h in range(mp // 2):
+        scores = recv_r[:, 2 * h:2 * h + 2, :, 0:chip_p].reshape(slots, chip_p)
+        logp = lp_perm[:, h * chip_p:(h + 1) * chip_p]
+        cross = cross + jnp.sum(jnp.exp(logp) * (logp - scores), axis=-1, keepdims=True)
+        mass = mass + jnp.sum(jnp.exp(scores), axis=-1, keepdims=True)
+    out_ref[...] = jnp.sum(place * cross, axis=0, keepdims=True) + jnp.log(
+        jnp.sum(place * mass, axis=0, keepdims=True)
+    )
+    for cp in copies:
+        cp.wait_send()
+
+
+def fused_device(query_hidden, query_proj, passages, teacher, neg_blocks):
+    dp, mp = lax.axis_size("dp"), lax.axis_size("mp")
+    qd, picks = neg_blocks.shape
+    qt = query_hidden.shape[1]
+    emb = query_proj.shape[1]
+    own_p, pt = passages.shape[0], passages.shape[1]
+    cap = max(2, -(-(qd * picks) // dp))
+    share = qt // mp
+    half = cap // 2
+    rows_b = half * share
+    names = neg_blocks.T
+    same = names[:, :, None, None] == names[None, None, :, :]
+    order = jnp.arange(qd, dtype=jnp.int32)
+    earlier = (order[None, :] < order[:, None])[None, :, None, :]
+    rank = jnp.sum((same & earlier).astype(jnp.int32), axis=(2, 3))
+    slotq = names * cap + rank
+    slote = (slotq[:, :, None] * share + jnp.arange(share, dtype=jnp.int32)).reshape(
+        picks, qd * share
+    )
+    vmem = pl.BlockSpec(memory_space=pltpu.VMEM)
+    dma = pltpu.SemaphoreType.DMA
+    loss = pl.pallas_call(
+        functools.partial(fused_kernel, dp, mp, cap),
+        out_shape=jax.ShapeDtypeStruct((1, qd), jnp.float32),
+        in_specs=[vmem] * 6,
+        out_specs=vmem,
+        scratch_shapes=[
+            pltpu.VMEM((mp, qd * share, emb), jnp.float32),
+            pltpu.VMEM((mp, qd * share, emb), jnp.bfloat16),
+            pltpu.VMEM((mp, qd * share, emb), jnp.bfloat16),
+            pltpu.VMEM((2, own_p * pt, emb), jnp.bfloat16),
+            pltpu.VMEM((dp, cap * share, qd * share), jnp.bfloat16),
+            pltpu.VMEM((dp, 2, rows_b, emb), jnp.bfloat16),
+            pltpu.VMEM((dp, mp, rows_b, emb), jnp.bfloat16),
+            pltpu.VMEM((2 * own_p, mp * rows_b), jnp.float32),
+            pltpu.VMEM((dp, half, 128), jnp.float32),
+            pltpu.VMEM((dp, mp, half, 128), jnp.float32),
+            pltpu.VMEM((dp * cap, teacher.shape[2]), jnp.float32),
+            dma((mp,)), dma((mp,)), dma, dma, dma((dp, 2)), dma((dp, 2)),
+            dma((dp,)), dma((dp,)), dma((dp, mp)), dma((dp, mp)),
+        ],
+        compiler_params=pltpu.CompilerParams(
+            collective_id=0, has_side_effects=True, vmem_limit_bytes=40 * 2**20
+        ),
+    )(query_hidden, query_proj, passages, teacher, slotq, slote)
+    return loss.reshape(qd)
 
 
 def soft_scores(slot_rows, passage_vecs):
@@ -44,19 +287,23 @@
     owner_hits = (owners[:, None] == jnp.arange(dp_count, dtype=jnp.int32)[None, :]).astype(
         jnp.int32
     )
-    earlier = jnp.cumsum(owner_hits, axis=0) - owner_hits
+    order = jnp.arange(row_count, dtype=jnp.int32)
+    before = (order[None, :] < order[:, None]).astype(jnp.float32)
+    earlier = jnp.dot(
+        before, owner_hits.astype(jnp.float32), preferred_element_type=jnp.float32
+    ).astype(jnp.int32)
     slot_rank = jnp.sum(earlier * owner_hits, axis=1)
     slot_ids = owners * capacity + slot_rank
     matches = (slot_ids[None, :] == jnp.arange(slots_all, dtype=jnp.int32)[:, None]).astype(
         jnp.int32
     )
-    row_query = jnp.arange(row_count, dtype=jnp.int32) // pick_count
-    source = jnp.sum(matches * row_query[None, :], axis=1)
-    filled = jnp.sum(matches, axis=1)
+    chosen = jnp.sum(matches.reshape(slots_all, query_count, pick_count), axis=2)
     token_share = lax.psum_scatter(partial_sum, "mp", scatter_dimension=1, tiled=True)
     share_vecs = unit_rows(token_share).astype(jnp.bfloat16)
     quarter = share_vecs.shape[1]
-    token_part = share_vecs[source] * filled[:, None, None].astype(jnp.bfloat16)
+    token_part = jnp.einsum(
+        "sq,qte->ste", chosen.astype(jnp.bfloat16), share_vecs, preferred_element_type=jnp.float32
+    ).astype(jnp.bfloat16)
     token_part = token_part.reshape(dp_count, capacity, quarter, embed_width)
     arrived = lax.all_to_all(token_part, "dp", split_axis=0, concat_axis=0, tiled=True)
     joined = lax.all_gather(arrived, "mp", axis=2, tiled=True)
@@ -83,6 +330,20 @@
         P("dp", None),
     )
     out_specs = P("dp")
-    return jax.shard_map(
-        per_device, mesh=mesh, in_specs=in_specs, out_specs=out_specs, check_vma=False
-    )
+    dp, mp = mesh.shape["dp"], mesh.shape["mp"]
+
+    def whole(query_hidden, query_proj, passages, teacher, neg_blocks):
+        qd, picks = neg_blocks.shape[0] // dp, neg_blocks.shape[1]
+        cap = max(2, -(-(qd * picks) // dp))
+        share = query_hidden.shape[1] // mp
+        own_p = passages.shape[0] // (dp * mp)
+        fits = (
+            mp == 4 and cap % 16 == 0 and share % 8 == 0 and own_p % group == 0
+            and dp * mp <= 64
+        )
+        return jax.shard_map(
+            fused_device if fits else per_device, mesh=mesh, in_specs=in_specs,
+            out_specs=out_specs, check_vma=False,
+        )(query_hidden, query_proj, passages, teacher, neg_blocks)
+
+    return whole

time: 114 us -> 41.4 us (0.36)
  waiting for transfers between devices: 44.1 us -> 0 us
  Pallas kernels: 0 us -> 36.6 us
  matrix products: 19.8 us -> 0 us
  blocking collectives: 19.8 us -> 0 us
  between operations: 13.6 us -> 0.05 us
  other arithmetic: 6.29 us -> 0.26 us
  starting transfers between devices: 5.56 us -> 0 us
    pallas_call x0 -> x1, Pallas kernels: none -> 36.6 us  [fused_device(): pl.pallas_call(functools.partial(fused_kernel, dp, mp, cap), out_shape=ja...]
    reduce_scatter x1 -> x0, waiting for transfers between devices: 23.8 us -> none  [per_device(): lax.psum_scatter(partial_sum, 'mp', scatter_dimension=1, tiled=True)]
    dot_general x9 -> x0, matrix products: 19.8 us -> none  [the longest x8 18 us: block_scores(): jnp.einsum('sie,pje->sipj', slot_block, passage_vecs, preferred_element_t...]
    all_to_all x1 -> x0, blocking collectives: 14.3 us -> none  [per_device(): lax.all_to_all(token_part, 'dp', split_axis=0, concat_axis=0, tiled=True)]
    all_gather x1 -> x0, waiting for transfers between devices: 13.8 us -> none  [per_device(): joined = lax.all_gather(arrived, 'mp', axis=2, tiled=True)]
    all_to_all x1 -> x0, waiting for transfers between devices: 6.5 us -> none  [per_device(): lax.all_to_all(scores, 'dp', split_axis=0, concat_axis=0, tiled=True)]
    all_to_all x1 -> x0, starting transfers between devices: 5.52 us -> none  [per_device(): lax.all_to_all(scores, 'dp', split_axis=0, concat_axis=0, tiled=True)]
    all_gather x1 -> x0, blocking collectives: 5.42 us -> none  [per_device(): student = lax.all_gather(home_scores, 'mp', axis=2, tiled=True)]
  transfers between devices with their start and end apart: 3 -> 0, of which waited for: 3 -> 0; matrix products, arithmetic and copies ran while one was open for 2% -> 0% of each run, Pallas kernels for 0% -> 0%
where the time goes in v1:
time: 41.4 us; the launch traced here: 41.1 us
  Pallas kernels  36.6 us (88%)
  local copies, waits for them, and re-layouts  4.17 us (10%)
    pallas_call x1, Pallas kernels, fused_device(): pl.pallas_call(functools.partial(fused_kernel, dp, mp, cap), out_shape=ja...  36.6 us
    unnamed x11, local copies, waits for them, and re-layouts  3.91 us

profile of v1, /device:TPU:0, one launch (start us, length us, event | category | flops | bytes accessed | tf_op | source)
XLA Modules:
  0.0 41.1 jit_solution(6415684364698202412)
XLA Ops:
  0.0 0.0 copy-start.4
  0.0 0.7 %copy-done.4 = s32[32,4]{0,1:T(4,128)S(1)} copy-done((s32[32,4]{0,1:T(4,128)S(1)}, s32[32,4]{0,1:T(4,128)}, u32[]{:S(2)}) %copy-start.4) | copy-done | bytes 536
  0.7 0.2 convert_reduce_fusion
  0.9 0.0 copy-start.3
  0.9 0.1 add.24
  1.0 0.0 copy-start.2
  1.0 0.1 add.25
  1.1 0.1 add.27
  1.2 0.5 %copy-done.3 = bf16[192,128]{1,0:T(8,128)(2,1)S(1)} copy-done((bf16[192,128]{1,0:T(8,128)(2,1)S(1)}, bf16[192,128]{1,0:T(8,128)(2,1)}, u32[]{:S(2)}) %copy-start.3) | copy-done | bytes 49176
  1.7 0.1 copy-done.2
  1.9 0.0 copy-start
  1.9 1.0 %copy-done = bf16[32,32,192]{2,1,0:T(8,128)(2,1)S(1)} copy-done((bf16[32,32,192]{2,1,0:T(8,128)(2,1)S(1)}, bf16[32,32,192]{2,1,0:T(8,128)(2,1)}, u32[]{:S(2)}) %copy-start) | copy-done | bytes 393240
  2.9 0.0 copy-start.1
  2.9 1.0 %copy-done.1 = bf16[16,128,128]{2,1,0:T(8,128)(2,1)S(1)} copy-done((bf16[16,128,128]{2,1,0:T(8,128)(2,1)S(1)}, bf16[16,128,128]{2,1,0:T(8,128)(2,1)}, u32[]{:S(2)}) %copy-start.1) | copy-done | bytes 524312
  4.0 36.6 %shard_map.55 = f32[1,32]{1,0:T(1,128)S(1)} custom-call(bf16[32,32,192]{2,1,0:T(8,128)(2,1)S(1)} %copy-done, bf16[192,128]{1,0:T(8,128)(2,1)S(1)} %copy-done.3, bf16[16,128,128]{2,1,0:T(8,128)(2,1)S(1)} %copy-done.1, f32[32,4,64]{2,1,0:T(4,128)S(1)} %copy-done.2, s32[4,32]{1,0:T(4,128)S(1)} %get-tuple-element.6.slotq_ref, ...), custom_call_target="tpu_custom_call" | custom-call | tf_op jit(solution)/shard_map/pallas_call | solution.py:229
  40.6 0.5 %copy.7 = f32[32]{0:T(128)} copy(f32[32]{0:T(128)S(1)} %bitcast.4) | data formatting | bytes 256
  (4 shorter events, 0.0 us)
Async XLA Ops:
  0.0 0.7 %copy-start.4 = (s32[32,4]{0,1:T(4,128)S(1)}, s32[32,4]{0,1:T(4,128)}, u32[]{:S(2)}) copy-start(s32[32,4]{0,1:T(4,128)} %param.9) | copy-start | bytes 1540
  0.9 0.8 %copy-start.3 = (bf16[192,128]{1,0:T(8,128)(2,1)S(1)}, bf16[192,128]{1,0:T(8,128)(2,1)}, u32[]{:S(2)}) copy-start(bf16[192,128]{1,0:T(8,128)(2,1)} %proj_ref.1) | copy-start | bytes 147460
  1.0 0.9 %copy-start.2 = (f32[32,4,64]{2,1,0:T(4,128)S(1)}, f32[32,4,64]{2,1,0:T(4,128)}, u32[]{:S(2)}) copy-start(f32[32,4,64]{2,1,0:T(4,128)} %teach_ref.1) | copy-start | bytes 98308
  1.9 1.0 %copy-start = (bf16[32,32,192]{2,1,0:T(8,128)(2,1)S(1)}, bf16[32,32,192]{2,1,0:T(8,128)(2,1)}, u32[]{:S(2)}) copy-start(bf16[32,32,192]{2,1,0:T(8,128)(2,1)} %hid_ref.1) | copy-start | bytes 1179652
  2.9 1.0 %copy-start.1 = (bf16[16,128,128]{2,1,0:T(8,128)(2,1)S(1)}, bf16[16,128,128]{2,1,0:T(8,128)(2,1)}, u32[]{:S(2)}) copy-start(bf16[16,128,128]{2,1,0:T(8,128)(2,1)} %pas_ref.1) | copy-start | bytes 1572868

commit v2 on v0

--- a/solution.py
+++ b/solution.py
@@ -1,13 +1,316 @@
+import functools
 import jax
 import jax.numpy as jnp
 from jax import lax
+from jax.experimental import pallas as pl
+from jax.experimental.pallas import tpu as pltpu
 from jax.sharding import PartitionSpec as P
 
 softness = 0.1
+log2_e = 1.4426950408889634
 
 
 def unit_rows(values):
     return values * lax.rsqrt(jnp.sum(values * values, axis=-1, keepdims=True) + 1e-06)
+
+
+def fused_kernel(
+    dp, mp, cap,
+    hid_hbm, proj_hbm, pas_hbm, teach_hbm, neg_hbm,
+    out_ref,
+    hid_ref, proj_ref, pas_ref, teach_ref, neg_ref,
+    part, send_a, recv_a, pvecs, pick, send_b, queries, sums, send_r, recv_r, lp_perm, place,
+    send_f, recv_f,
+    loads, a_send, a_recv, p_send, p_recv, b_send, b_recv, r_send, r_recv, f_send, f_recv,
+):
+    d = lax.axis_index("dp")
+    m = lax.axis_index("mp")
+    x, c = m // 2, m % 2
+    sib, across = 2 * x + 1 - c, 2 * (1 - x) + c
+    far = 2 * (1 - x) + 1 - c
+    qd, qt = hid_ref.shape[0], hid_ref.shape[1]
+    emb = proj_ref.shape[1]
+    picks = teach_ref.shape[1]
+    share = qt // mp
+    quarter = cap // mp
+    rows_b = quarter * share
+    own_p, pt = pas_ref.shape[0], pas_ref.shape[1]
+    block_p = own_p * mp
+    pairs = dp // 2
+
+    def remote(src, dst, ssem, rsem, dd, mm):
+        return pltpu.make_async_remote_copy(
+            src_ref=src, dst_ref=dst, send_sem=ssem, recv_sem=rsem,
+            device_id=(dd, mm), device_id_type=pl.DeviceIdType.MESH,
+        )
+
+    def partner(g, e, back):
+        pair = (d // 2 - g + pairs) % pairs if back else (d // 2 + g) % pairs
+        return 2 * pair + (d % 2 + e) % 2
+
+    barrier = pltpu.get_barrier_semaphore()
+    for j in range(dp):
+        for i in range(mp):
+            if j or i:
+                pl.semaphore_signal(
+                    barrier, inc=1, device_id=((d + j) % dp, (m + i) % mp),
+                    device_id_type=pl.DeviceIdType.MESH,
+                )
+    inputs = []
+    for k, (src, dst) in enumerate((
+        (hid_hbm, hid_ref), (proj_hbm, proj_ref), (neg_hbm, neg_ref), (pas_hbm, pas_ref),
+        (teach_hbm, teach_ref),
+    )):
+        cp = pltpu.make_async_copy(src, dst, loads.at[k])
+        cp.start()
+        inputs.append(cp)
+
+    inputs[0].wait()
+    inputs[1].wait()
+    projected = jnp.dot(
+        hid_ref[...].reshape(qd * qt, hid_ref.shape[2]), proj_ref[...],
+        preferred_element_type=jnp.float32,
+    ).reshape(qd, qt, emb)
+    for k in range(mp):
+        piece = projected[:, k * share:(k + 1) * share, :].reshape(qd * share, emb)
+        part[k] = piece
+        send_a[k] = piece.astype(jnp.bfloat16)
+    inputs[3].wait()
+    pvecs[m] = unit_rows(pas_ref[...].reshape(own_p * pt, emb).astype(jnp.float32)).astype(
+        jnp.bfloat16
+    )
+
+    pl.semaphore_wait(barrier, dp * mp - 1)
+
+    copies = []
+    for i in range(1, mp):
+        to = (m + i) % mp
+        cp = remote(send_a.at[to], recv_a.at[m], a_send.at[i], a_recv.at[m], d, to)
+        cp.start()
+        copies.append(cp)
+    for i, to in ((0, across), (1, sib)):
+        cp = remote(pvecs.at[m], pvecs.at[m], p_send.at[i], p_recv.at[m], d, to)
+        cp.start()
+        copies.append(cp)
+
+    inputs[2].wait()
+    owner = lax.broadcasted_iota(jnp.int32, (qd, dp), 1)
+    hits = [
+        jnp.where(neg_ref[:, k:k + 1] == owner, 1.0, 0.0) for k in range(picks)
+    ]
+    row_q = lax.broadcasted_iota(jnp.int32, (qd, qd), 0)
+    lane_q = lax.broadcasted_iota(jnp.int32, (qd, qd), 1)
+    same = jnp.where(row_q == lane_q, 1.0, 0.0)
+    before = jnp.where(row_q < lane_q, 1.0, 0.0)
+
+    def turned(left, right):
+        return lax.dot_general(
+            left, right, (((0,), (0,)), ((), ())), preferred_element_type=jnp.float32
+        )
+
+    hits_t = [turned(h, same) for h in hits]
+    rank = turned(sum(hits), before)
+    code = jnp.where(sum(hits_t) > 0.5, rank, -1.0)
+    spread = jnp.where(
+        lax.broadcasted_iota(jnp.int32, (qd, qd * share), 1) // share
+        == lax.broadcasted_iota(jnp.int32, (qd, qd * share), 0), 1.0, 0.0,
+    )
+    code_wide = jnp.dot(code, spread, preferred_element_type=jnp.float32)
+    token = (lax.broadcasted_iota(jnp.int32, (dp, qd * share), 1) % share).astype(jnp.float32)
+    code_wide = jnp.round(code_wide) * share + token
+    row = lax.broadcasted_iota(jnp.int32, (cap * share, qd * share), 0).astype(jnp.float32)
+    for b in range(dp):
+        pick[b] = jnp.where(code_wide[b:b + 1, :] == row, 1.0, 0.0).astype(jnp.bfloat16)
+
+    total = part[m]
+    for i in range(1, mp):
+        src = (m + i) % mp
+        remote(send_a.at[src], recv_a.at[src], a_send.at[i], a_recv.at[src], d, src).wait_recv()
+        total = total + recv_a[src].astype(jnp.float32)
+    share_vecs = unit_rows(total).astype(jnp.bfloat16)
+
+    for g in range(pairs):
+        for e in range(2):
+            b = partner(g, e, False)
+            chosen = jnp.dot(pick[b], share_vecs, preferred_element_type=jnp.float32).astype(
+                jnp.bfloat16
+            )
+            send_b[2 * g + e] = chosen.reshape(mp, rows_b, emb)
+            for i in range(mp):
+                to = (m + i) % mp
+                if g == 0 and e == 0 and i == 0:
+                    queries[d, m] = send_b[0, m]
+                    continue
+                cp = remote(
+                    send_b.at[2 * g + e, to], queries.at[d, m], b_send.at[2 * g + e, i],
+                    b_recv.at[d, m], b, to,
+                )
+                cp.start()
+                copies.append(cp)
+
+    inputs[4].wait()
+    norm = jnp.zeros((qd, 1), jnp.float32)
+    for k in range(picks):
+        norm = norm + jnp.sum(jnp.exp(teach_ref[:, k, :]), axis=-1, keepdims=True)
+    log_norm = jnp.log(norm)
+    local = lax.broadcasted_iota(jnp.int32, (8, qd), 0)
+    wanted = jnp.where(local < quarter, local + m * quarter, cap).astype(jnp.float32)
+    perm = jnp.zeros((dp * 8, teach_ref.shape[2]), jnp.float32)
+    spots = [jnp.where(code[b:b + 1, :] == wanted, 1.0, 0.0) for b in range(dp)]
+    place[...] = jnp.concatenate(spots, axis=0)
+    for k in range(picks):
+        here = jnp.concatenate(
+            [spots[b] * hits_t[k][b:b + 1, :] for b in range(dp)], axis=0
+        )
+        perm = perm + jnp.dot(
+            here, teach_ref[:, k, :] - log_norm, precision=lax.Precision.HIGHEST,
+            preferred_element_type=jnp.float32,
+        )
+    lp_perm[...] = perm
+
+    lanes = mp * rows_b
+    lane = lax.broadcasted_iota(jnp.int32, (16, 2 * lanes), 1)
+    slot_of = lax.broadcasted_iota(jnp.int32, (16, 2 * lanes), 0)
+    fold = jnp.where((lane // lanes) * 8 + (lane // share) % quarter == slot_of, 1.0, 0.0)
+
+    def arrive(g):
+        for e in range(2):
+            src_d = partner(g, e, True)
+            for i in range(mp):
+                if g == 0 and e == 0 and i == 0:
+                    continue
+                src = (m + i) % mp
+                remote(
+                    send_b.at[2 * g + e, src], queries.at[src_d, src], b_send.at[2 * g + e, i],
+                    b_recv.at[src_d, src], src_d, src,
+                ).wait_recv()
+
+    def score(g, side):
+        tokens = jnp.concatenate(
+            [queries[partner(g, e, True)].reshape(lanes, emb) for e in range(2)], axis=0
+        )
+
+        def one(h, carry):
+            at = 2 * side + h
+            sims = lax.dot_general(
+                pvecs[at], tokens, (((1,), (1,)), ((), ())), preferred_element_type=jnp.float32
+            )
+            weights = jnp.exp2(sims * (log2_e / softness)).reshape(own_p, pt, 2 * lanes)
+            sums[g, pl.ds(pl.multiple_of(at * own_p, own_p), own_p), :] = jnp.sum(weights, axis=1)
+            return carry
+
+        lax.fori_loop(0, 2, one, 0)
+
+    def passages_from(src):
+        remote(pvecs.at[src], pvecs.at[src], p_send.at[0], p_recv.at[src], d, across).wait_recv()
+
+    arrive(0)
+    passages_from(sib)
+    score(0, x)
+    for g in range(1, pairs):
+        arrive(g)
+        if g == min(2, pairs - 1):
+            passages_from(across)
+            cp = remote(pvecs.at[across], pvecs.at[across], p_send.at[2], p_recv.at[across], d, sib)
+            cp.start()
+            copies.append(cp)
+        score(g, x)
+    passages_from(far)
+    for g in range(pairs):
+        score(g, 1 - x)
+        soft = softness * jnp.log(sums[g])
+        student = lax.dot_general(
+            fold, soft, (((1,), (1,)), ((), ())), precision=lax.Precision.HIGHEST,
+            preferred_element_type=jnp.float32,
+        )
+        for e in range(2):
+            piece = student[8 * e:8 * e + 8, :]
+            if g == 0 and e == 0:
+                recv_r[d, :, 0:block_p] = piece
+                continue
+            send_r[2 * g + e, :, 0:block_p] = piece
+            cp = remote(
+                send_r.at[2 * g + e], recv_r.at[d], r_send.at[2 * g + e], r_recv.at[d],
+                partner(g, e, True), m,
+            )
+            cp.start()
+            copies.append(cp)
+
+    for g in range(pairs):
+        for e in range(2):
+            if g or e:
+                b = partner(g, e, False)
+                remote(
+                    send_r.at[2 * g + e], recv_r.at[b], r_send.at[2 * g + e], r_recv.at[b], b, m
+                ).wait_recv()
+
+    scores = recv_r[:, :, 0:block_p].reshape(dp * 8, block_p)
+    logp = lp_perm[...]
+    cross = jnp.sum(jnp.exp(logp) * (logp - scores), axis=-1, keepdims=True)
+    mass = jnp.sum(jnp.exp(scores), axis=-1, keepdims=True)
+    send_f[0:1, 0:qd] = jnp.sum(place[...] * cross, axis=0, keepdims=True)
+    send_f[1:2, 0:qd] = jnp.sum(place[...] * mass, axis=0, keepdims=True)
+    for i in range(1, mp):
+        to = (m + i) % mp
+        cp = remote(send_f, recv_f.at[m], f_send.at[i], f_recv.at[m], d, to)
+        cp.start()
+        copies.append(cp)
+    cross_q, mass_q = send_f[0:1, 0:qd], send_f[1:2, 0:qd]
+    for i in range(1, mp):
+        src = (m + i) % mp
+        remote(send_f, recv_f.at[src], f_send.at[i], f_recv.at[src], d, src).wait_recv()
+        cross_q = cross_q + recv_f[src, 0:1, 0:qd]
+        mass_q = mass_q + recv_f[src, 1:2, 0:qd]
+    out_ref[...] = cross_q + jnp.log(mass_q)
+    for cp in copies:
+        cp.wait_send()
+
+
+def fused_device(query_hidden, query_proj, passages, teacher, neg_blocks):
+    dp, mp = lax.axis_size("dp"), lax.axis_size("mp")
+    qd, picks = neg_blocks.shape
+    qt = query_hidden.shape[1]
+    emb = query_proj.shape[1]
+    own_p, pt = passages.shape[0], passages.shape[1]
+    cap = max(2, -(-(qd * picks) // dp))
+    share = qt // mp
+    rows_b = cap // mp * share
+    anywhere = pl.BlockSpec(memory_space=pl.ANY)
+    dma = pltpu.SemaphoreType.DMA
+    f32, bf16 = jnp.float32, jnp.bfloat16
+    loss = pl.pallas_call(
+        functools.partial(fused_kernel, dp, mp, cap),
+        out_shape=jax.ShapeDtypeStruct((1, qd), f32),
+        in_specs=[anywhere] * 5,
+        out_specs=pl.BlockSpec(memory_space=pltpu.VMEM),
+        scratch_shapes=[
+            pltpu.VMEM(query_hidden.shape, bf16),
+            pltpu.VMEM(query_proj.shape, bf16),
+            pltpu.VMEM(passages.shape, bf16),
+            pltpu.VMEM(teacher.shape, f32),
+            pltpu.VMEM(neg_blocks.shape, jnp.int32),
+            pltpu.VMEM((mp, qd * share, emb), f32),
+            pltpu.VMEM((mp, qd * share, emb), bf16),
+            pltpu.VMEM((mp, qd * share, emb), bf16),
+            pltpu.VMEM((mp, own_p * pt, emb), bf16),
+            pltpu.VMEM((dp, cap * share, qd * share), bf16),
+            pltpu.VMEM((dp, mp, rows_b, emb), bf16),
+            pltpu.VMEM((dp, mp, rows_b, emb), bf16),
+            pltpu.VMEM((dp // 2, mp * own_p, 2 * mp * rows_b), f32),
+            pltpu.VMEM((dp, 8, 128), f32),
+            pltpu.VMEM((dp, 8, 128), f32),
+            pltpu.VMEM((dp * 8, teacher.shape[2]), f32),
+            pltpu.VMEM((dp * 8, qd), f32),
+            pltpu.VMEM((8, 128), f32),
+            pltpu.VMEM((mp, 8, 128), f32),
+            dma((5,)), dma((mp,)), dma((mp,)), dma((3,)), dma((mp,)), dma((dp, mp)),
+            dma((dp, mp)), dma((dp,)), dma((dp,)), dma((mp,)), dma((mp,)),
+        ],
+        compiler_params=pltpu.CompilerParams(
+            collective_id=0, has_side_effects=True, vmem_limit_bytes=60 * 2**20
+        ),
+    )(query_hidden, query_proj, passages, teacher, neg_blocks)
+    return loss.reshape(qd)
 
 
 def soft_scores(slot_rows, passage_vecs):
@@ -44,19 +347,23 @@
     owner_hits = (owners[:, None] == jnp.arange(dp_count, dtype=jnp.int32)[None, :]).astype(
         jnp.int32
     )
-    earlier = jnp.cumsum(owner_hits, axis=0) - owner_hits
+    order = jnp.arange(row_count, dtype=jnp.int32)
+    before = (order[None, :] < order[:, None]).astype(jnp.float32)
+    earlier = jnp.dot(
+        before, owner_hits.astype(jnp.float32), preferred_element_type=jnp.float32
+    ).astype(jnp.int32)
     slot_rank = jnp.sum(earlier * owner_hits, axis=1)
     slot_ids = owners * capacity + slot_rank
     matches = (slot_ids[None, :] == jnp.arange(slots_all, dtype=jnp.int32)[:, None]).astype(
         jnp.int32
     )
-    row_query = jnp.arange(row_count, dtype=jnp.int32) // pick_count
-    source = jnp.sum(matches * row_query[None, :], axis=1)
-    filled = jnp.sum(matches, axis=1)
+    chosen = jnp.sum(matches.reshape(slots_all, query_count, pick_count), axis=2)
     token_share = lax.psum_scatter(partial_sum, "mp", scatter_dimension=1, tiled=True)
     share_vecs = unit_rows(token_share).astype(jnp.bfloat16)
     quarter = share_vecs.shape[1]
-    token_part = share_vecs[source] * filled[:, None, None].astype(jnp.bfloat16)
+    token_part = jnp.einsum(
+        "sq,qte->ste", chosen.astype(jnp.bfloat16), share_vecs, preferred_element_type=jnp.float32
+    ).astype(jnp.bfloat16)
     token_part = token_part.reshape(dp_count, capacity, quarter, embed_width)
     arrived = lax.all_to_all(token_part, "dp", split_axis=0, concat_axis=0, tiled=True)
     joined = lax.all_gather(arrived, "mp", axis=2, tiled=True)
@@ -83,6 +390,21 @@
         P("dp", None),
     )
     out_specs = P("dp")
-    return jax.shard_map(
-        per_device, mesh=mesh, in_specs=in_specs, out_specs=out_specs, check_vma=False
-    )
+    dp, mp = mesh.shape["dp"], mesh.shape["mp"]
+
+    def whole(query_hidden, query_proj, passages, teacher, neg_blocks):
+        qd, picks = neg_blocks.shape[0] // dp, neg_blocks.shape[1]
+        cap = max(2, -(-(qd * picks) // dp))
+        share = query_hidden.shape[1] // mp
+        own_p = passages.shape[0] // (dp * mp)
+        fits = (
+            mp == 4 and dp % 2 == 0 and dp * mp <= 64 and share % 8 == 0
+            and cap % mp == 0 and cap // mp <= 8 and (cap // mp * share) % 16 == 0
+            and own_p % 8 == 0 and own_p * mp <= 128 and cap <= 256
+        )
+        return jax.shard_map(
+            fused_device if fits else per_device, mesh=mesh, in_specs=in_specs,
+            out_specs=out_specs, check_vma=False,
+        )(query_hidden, query_proj, passages, teacher, neg_blocks)
+
+    return whole

time: 114 us -> 43.9 us (0.39)
  waiting for transfers between devices: 44.1 us -> 0 us
  Pallas kernels: 0 us -> 41.3 us
  matrix products: 19.8 us -> 0 us
  blocking collectives: 19.8 us -> 0 us
  between operations: 13.6 us -> 0.02 us
  other arithmetic: 6.29 us -> 0 us
  starting transfers between devices: 5.56 us -> 0 us
  local copies, waits for them, and re-layouts: 4.37 us -> 2.49 us
    pallas_call x0 -> x1, Pallas kernels: none -> 41.3 us  [fused_device(): pl.pallas_call(functools.partial(fused_kernel, dp, mp, cap), out_shape=ja...]
    reduce_scatter x1 -> x0, waiting for transfers between devices: 23.8 us -> none  [per_device(): lax.psum_scatter(partial_sum, 'mp', scatter_dimension=1, tiled=True)]
    dot_general x9 -> x0, matrix products: 19.8 us -> none  [the longest x8 18 us: block_scores(): jnp.einsum('sie,pje->sipj', slot_block, passage_vecs, preferred_element_t...]
    all_to_all x1 -> x0, blocking collectives: 14.3 us -> none  [per_device(): lax.all_to_all(token_part, 'dp', split_axis=0, concat_axis=0, tiled=True)]
    all_gather x1 -> x0, waiting for transfers between devices: 13.8 us -> none  [per_device(): joined = lax.all_gather(arrived, 'mp', axis=2, tiled=True)]
    all_to_all x1 -> x0, waiting for transfers between devices: 6.5 us -> none  [per_device(): lax.all_to_all(scores, 'dp', split_axis=0, concat_axis=0, tiled=True)]
    all_to_all x1 -> x0, starting transfers between devices: 5.52 us -> none  [per_device(): lax.all_to_all(scores, 'dp', split_axis=0, concat_axis=0, tiled=True)]
    all_gather x1 -> x0, blocking collectives: 5.42 us -> none  [per_device(): student = lax.all_gather(home_scores, 'mp', axis=2, tiled=True)]
  transfers between devices with their start and end apart: 3 -> 0, of which waited for: 3 -> 0; matrix products, arithmetic and copies ran while one was open for 2% -> 0% of each run, Pallas kernels for 0% -> 0%
where the time goes in v2:
time: 43.9 us; the launch traced here: 43.8 us
  Pallas kernels  41.3 us (94%)
  local copies, waits for them, and re-layouts  2.49 us (6%)
    pallas_call x1, Pallas kernels, fused_device(): pl.pallas_call(functools.partial(fused_kernel, dp, mp, cap), out_shape=ja...  41.3 us
    unnamed x4, local copies, waits for them, and re-layouts  2.49 us

profile of v2, /device:TPU:0, one launch (start us, length us, event | category | flops | bytes accessed | tf_op | source)
XLA Modules:
  0.0 43.8 jit_solution(5457752444352112060)
XLA Ops:
  0.0 1.4 %copy.6.neg_hbm = s32[32,4]{1,0:T(8,128)} copy(s32[32,4]{0,1:T(4,128)} %param.9) | data formatting | bytes 1024 | tf_op args[4]
  1.4 41.3 %shard_map.55 = f32[1,32]{1,0:T(1,128)} custom-call(bf16[32,32,192]{2,1,0:T(8,128)(2,1)} %hid_hbm.1, bf16[192,128]{1,0:T(8,128)(2,1)} %proj_hbm.1, bf16[16,128,128]{2,1,0:T(8,128)(2,1)} %pas_hbm.1, f32[32,4,64]{2,1,0:T(4,128)} %teach_hbm.1, s32[32,4]{1,0:T(8,128)} %copy.6.neg_hbm), custom_call_target="tpu_custom_call" | custom-call | tf_op jit(solution)/shard_map/pallas_call | solution.py:281
  42.6 0.0 copy-start
  42.6 0.6 %copy-done = f32[1,32]{1,0:T(1,128)S(1)} copy-done((f32[1,32]{1,0:T(1,128)S(1)}, f32[1,32]{1,0:T(1,128)}, u32[]{:S(2)}) %copy-start) | copy-done | bytes 152
  43.3 0.5 %copy.8 = f32[32]{0:T(128)} copy(f32[32]{0:T(128)S(1)} %bitcast.1) | data formatting | bytes 256
Async XLA Ops:
  42.6 0.6 %copy-start = (f32[1,32]{1,0:T(1,128)S(1)}, f32[1,32]{1,0:T(1,128)}, u32[]{:S(2)}) copy-start(f32[1,32]{1,0:T(1,128)} %shard_map.55) | copy-start | bytes 388

commit v3 on v1

v3 whole, which is shorter than its diff:
```python
import functools
import jax
import jax.numpy as jnp
from jax import lax
from jax.experimental import pallas as pl
from jax.experimental.pallas import tpu as pltpu
from jax.sharding import PartitionSpec as P

softness = 0.1
log2_e = 1.4426950408889634


def unit_rows(values):
    return values * lax.rsqrt(jnp.sum(values * values, axis=-1, keepdims=True) + 1e-06)


def fused_kernel(
    dp, mp, cap,
    hid_hbm, proj_hbm, pas_hbm, teach_hbm, neg_hbm,
    out_ref,
    hid_ref, proj_ref, pas_ref, teach_ref, neg_ref,
    part, send_a, recv_a, pvecs, pick, send_b, queries, sums, send_r, recv_r, lp_perm, place,
    loads, a_send, a_recv, p_send, p_recv, b_send, b_recv, c_send, c_recv, r_send, r_recv,
):
    d = lax.axis_index("dp")
    m = lax.axis_index("mp")
    x, c = m // 2, m % 2
    sib, across = 2 * x + 1 - c, 2 * (1 - x) + c
    qd, qt = hid_ref.shape[0], hid_ref.shape[1]
    emb = proj_ref.shape[1]
    picks = teach_ref.shape[1]
    share = qt // mp
    half = cap // 2
    rows_b = half * share
    own_p, pt = pas_ref.shape[0], pas_ref.shape[1]
    chip_p = 2 * own_p
    slots = dp * cap
    direct = min(2, dp)

    def remote(src, dst, ssem, rsem, dd, mm):
        return pltpu.make_async_remote_copy(
            src_ref=src, dst_ref=dst, send_sem=ssem, recv_sem=rsem,
            device_id=(dd, mm), device_id_type=pl.DeviceIdType.MESH,
        )

    def partner(j):
        at, bit = d, 1
        while bit <= j:
            if j & bit:
                at = at + bit - 2 * bit * ((d // bit) % 2)
            bit = 2 * bit
        return at

    barrier = pltpu.get_barrier_semaphore()
    for j in range(dp):
        for i in range(mp):
            if j or i:
                pl.semaphore_signal(
                    barrier, inc=1, device_id=((d + j) % dp, (m + i) % mp),
                    device_id_type=pl.DeviceIdType.MESH,
                )
    inputs = []
    for k, (src, dst) in enumerate((
        (hid_hbm, hid_ref), (proj_hbm, proj_ref), (neg_hbm, neg_ref), (pas_hbm, pas_ref),
        (teach_hbm, teach_ref),
    )):
        cp = pltpu.make_async_copy(src, dst, loads.at[k])
        cp.start()
        inputs.append(cp)

    inputs[0].wait()
    inputs[1].wait()
    projected = jnp.dot(
        hid_ref[...].reshape(qd * qt, hid_ref.shape[2]), proj_ref[...],
        preferred_element_type=jnp.float32,
    ).reshape(qd, qt, emb)
    for k in range(mp):
        piece = projected[:, k * share:(k + 1) * share, :].reshape(qd * share, emb)
        part[k] = piece
        send_a[k] = piece.astype(jnp.bfloat16)
    inputs[3].wait()
    pvecs[c] = unit_rows(pas_ref[...].reshape(own_p * pt, emb).astype(jnp.float32)).astype(
        jnp.bfloat16
    )

    pl.semaphore_wait(barrier, dp * mp - 1)

    copies = []
    for i in range(1, mp):
        to = (m + i) % mp
        cp = remote(send_a.at[to], recv_a.at[m], a_send.at[i], a_recv.at[m], d, to)
        cp.start()
        copies.append(cp)
    cp = remote(pvecs.at[c], pvecs.at[c], p_send, p_recv, d, sib)
    cp.start()
    copies.append(cp)

    inputs[2].wait()
    owner = lax.broadcasted_iota(jnp.int32, (dp, qd), 0)
    hits_t = [jnp.where(neg_ref[k:k + 1, :] == owner, 1.0, 0.0) for k in range(picks)]
    before = jnp.where(
        lax.broadcasted_iota(jnp.int32, (qd, qd), 0)
        < lax.broadcasted_iota(jnp.int32, (qd, qd), 1), 1.0, 0.0,
    )
    rank = jnp.dot(sum(hits_t), before, preferred_element_type=jnp.float32)
    code = jnp.where(sum(hits_t) > 0.5, rank, -1.0)
    spread = jnp.where(
        lax.broadcasted_iota(jnp.int32, (qd, qd * share), 1) // share
        == lax.broadcasted_iota(jnp.int32, (qd, qd * share), 0), 1.0, 0.0,
    )
    code_wide = jnp.dot(code, spread, preferred_element_type=jnp.float32)
    token = (lax.broadcasted_iota(jnp.int32, (dp, qd * share), 1) % share).astype(jnp.float32)
    code_wide = jnp.round(code_wide) * share + token
    row = lax.broadcasted_iota(jnp.int32, (cap * share, qd * share), 0).astype(jnp.float32)
    for b in range(dp):
        pick[b] = jnp.where(code_wide[b:b + 1, :] == row, 1.0, 0.0).astype(jnp.bfloat16)

    peers = ((m, c), (sib, 1 - c), (across, c), (2 * (1 - x) + 1 - c, 1 - c))
    total = part[m]
    for i in range(1, mp):
        src = (m + i) % mp
        remote(send_a.at[src], recv_a.at[src], a_send.at[i], a_recv.at[src], d, src).wait_recv()
        total = total + recv_a[src].astype(jnp.float32)
    share_vecs = unit_rows(total).astype(jnp.bfloat16)

    for j in range(dp):
        b = partner(j)
        chosen = jnp.dot(pick[b], share_vecs, preferred_element_type=jnp.float32).astype(
            jnp.bfloat16
        )
        send_b[j] = chosen.reshape(2, rows_b, emb)
        for i, (to, half_of) in enumerate(peers[:mp if j < direct else 2]):
            if j == 0 and i == 0:
                queries[d, m] = send_b[0, c]
                continue
            cp = remote(
                send_b.at[j, half_of], queries.at[d, m], b_send.at[j, i], b_recv.at[d, m], b, to
            )
            cp.start()
            copies.append(cp)

    inputs[4].wait()
    norm = jnp.zeros((qd, 1), jnp.float32)
    for k in range(picks):
        norm = norm + jnp.sum(jnp.exp(teach_ref[:, k, :]), axis=-1, keepdims=True)
    log_norm = jnp.log(norm)
    local = lax.broadcasted_iota(jnp.int32, (cap, qd), 0).astype(jnp.float32)
    perm = jnp.zeros((slots, teach_ref.shape[2]), jnp.float32)
    spots = [jnp.where(code[b:b + 1, :] == local, 1.0, 0.0) for b in range(dp)]
    place[...] = jnp.concatenate(spots, axis=0)
    for k in range(picks):
        here = jnp.concatenate(
            [spots[b] * hits_t[k][b:b + 1, :] for b in range(dp)], axis=0
        )
        perm = perm + jnp.dot(
            here, teach_ref[:, k, :] - log_norm, precision=lax.Precision.HIGHEST,
            preferred_element_type=jnp.float32,
        )
    lp_perm[...] = perm

    lanes = mp * rows_b
    lane = lax.broadcasted_iota(jnp.int32, (half, lanes), 1)
    slot_of = lax.broadcasted_iota(jnp.int32, (half, lanes), 0)
    fold = jnp.where((lane // share) % half == slot_of, 1.0, 0.0)

    def arrive(j):
        src_d = partner(j)
        for i, (src, _) in enumerate(peers[:mp if j < direct else 2]):
            if j == 0 and i == 0:
                continue
            remote(
                send_b.at[j, 0], queries.at[src_d, src], b_send.at[j, i], b_recv.at[src_d, src],
                src_d, src,
            ).wait_recv()
        if j >= direct:
            mine = queries.at[src_d, pl.ds(2 * x, 2)]
            fwd = remote(mine, mine, c_send.at[j], c_recv.at[src_d], d, across)
            fwd.start()
            copies.append(fwd)

    def complete(j):
        if j >= direct:
            src_d = partner(j)
            other = queries.at[src_d, pl.ds(2 * (1 - x), 2)]
            remote(other, other, c_send.at[j], c_recv.at[src_d], d, across).wait_recv()

    def score(j):
        tokens = queries[partner(j)].reshape(lanes, emb)

        def one(at, carry):
            sims = lax.dot_general(
                pvecs[at], tokens, (((1,), (1,)), ((), ())), preferred_element_type=jnp.float32
            )
            weights = jnp.exp2(sims * (log2_e / softness)).reshape(own_p, pt, lanes)
            sums[pl.ds(pl.multiple_of(at * own_p, own_p), own_p), :] = jnp.sum(weights, axis=1)
            return carry

        lax.fori_loop(0, 2, one, 0)

    arrive(0)
    remote(pvecs.at[1 - c], pvecs.at[1 - c], p_send, p_recv, d, sib).wait_recv()
    ahead = 1
    for j in range(dp):
        while ahead < dp and ahead <= j + 2:
            arrive(ahead)
            ahead = ahead + 1
        complete(j)
        score(j)
        soft = softness * jnp.log(sums[...])
        student = lax.dot_general(
            fold, soft, (((1,), (1,)), ((), ())), precision=lax.Precision.HIGHEST,
            preferred_element_type=jnp.float32,
        )
        send_r[j, :, 0:chip_p] = student
        for i in range(mp):
            to = (m + i) % mp
            if j == 0 and i == 0:
                recv_r[d, m, :, 0:chip_p] = student
                continue
            cp = remote(
                send_r.at[j], recv_r.at[d, m], r_send.at[j, i], r_recv.at[d, m], partner(j), to
            )
            cp.start()
            copies.append(cp)

    for j in range(dp):
        b = partner(j)
        for i in range(mp):
            if j or i:
                src = (m + i) % mp
                remote(
                    send_r.at[j], recv_r.at[b, src], r_send.at[j, i], r_recv.at[b, src], b, src
                ).wait_recv()

    cross = jnp.zeros((slots, 1), jnp.float32)
    mass = jnp.zeros((slots, 1), jnp.float32)
    for h in range(mp // 2):
        scores = recv_r[:, 2 * h:2 * h + 2, :, 0:chip_p].reshape(slots, chip_p)
        logp = lp_perm[:, h * chip_p:(h + 1) * chip_p]
        cross = cross + jnp.sum(jnp.exp(logp) * (logp - scores), axis=-1, keepdims=True)
        mass = mass + jnp.sum(jnp.exp(scores), axis=-1, keepdims=True)
    out_ref[...] = jnp.sum(place[...] * cross, axis=0, keepdims=True) + jnp.log(
        jnp.sum(place[...] * mass, axis=0, keepdims=True)
    )
    for cp in copies:
        cp.wait_send()


def fused_device(query_hidden, query_proj, passages, teacher, neg_blocks):
    dp, mp = lax.axis_size("dp"), lax.axis_size("mp")
    qd, picks = neg_blocks.shape
    qt = query_hidden.shape[1]
    emb = query_proj.shape[1]
    own_p, pt = passages.shape[0], passages.shape[1]
    cap = max(2, -(-(qd * picks) // dp))
    share = qt // mp
    half = cap // 2
    rows_b = half * share
    anywhere = pl.BlockSpec(memory_space=pl.ANY)
    dma = pltpu.SemaphoreType.DMA
    f32, bf16 = jnp.float32, jnp.bfloat16
    loss = pl.pallas_call(
        functools.partial(fused_kernel, dp, mp, cap),
        out_shape=jax.ShapeDtypeStruct((1, qd), f32),
        in_specs=[anywhere] * 5,
        out_specs=pl.BlockSpec(memory_space=pltpu.VMEM),
        scratch_shapes=[
            pltpu.VMEM(query_hidden.shape, bf16),
            pltpu.VMEM(query_proj.shape, bf16),
            pltpu.VMEM(passages.shape, bf16),
            pltpu.VMEM(teacher.shape, f32),
            pltpu.VMEM((picks, qd), jnp.int32),
            pltpu.VMEM((mp, qd * share, emb), f32),
            pltpu.VMEM((mp, qd * share, emb), bf16),
            pltpu.VMEM((mp, qd * share, emb), bf16),
            pltpu.VMEM((2, own_p * pt, emb), bf16),
            pltpu.VMEM((dp, cap * share, qd * share), bf16),
            pltpu.VMEM((dp, 2, rows_b, emb), bf16),
            pltpu.VMEM((dp, mp, rows_b, emb), bf16),
            pltpu.VMEM((2 * own_p, mp * rows_b), f32),
            pltpu.VMEM((dp, half, 128), f32),
            pltpu.VMEM((dp, mp, half, 128), f32),
            pltpu.VMEM((dp * cap, teacher.shape[2]), f32),
            pltpu.VMEM((dp * cap, qd), f32),
            dma((5,)), dma((mp,)), dma((mp,)), dma, dma, dma((dp, mp)), dma((dp, mp)),
            dma((dp,)), dma((dp,)), dma((dp, mp)), dma((dp, mp)),
        ],
        compiler_params=pltpu.CompilerParams(
            collective_id=0, has_side_effects=True, vmem_limit_bytes=60 * 2**20
        ),
    )(query_hidden, query_proj, passages, teacher, neg_blocks.T)
    return loss.reshape(qd)


def soft_scores(slot_rows, passage_vecs):
    slot_count = slot_rows.shape[0]
    block_size = 16
    padded_count = -(-slot_count // block_size) * block_size
    blocked = slot_rows.reshape(
        padded_count // block_size, block_size, slot_rows.shape[1], slot_rows.shape[2]
    )

    def block_scores(slot_block):
        sims = jnp.einsum(
            "sie,pje->sipj", slot_block, passage_vecs, preferred_element_type=jnp.float32
        )
        softened = softness * jnp.log(jnp.sum(jnp.exp(sims / softness), axis=-1))
        return jnp.sum(softened, axis=1)

    scored = lax.map(block_scores, blocked)
    return scored.reshape(padded_count, -1)


def per_device(query_hidden, query_proj, passages, teacher, neg_blocks):
    partial_sum = jnp.einsum(
        "qth,he->qte", query_hidden, query_proj, preferred_element_type=jnp.float32
    )
    passage_vecs = unit_rows(passages.astype(jnp.float32)).astype(jnp.bfloat16)
    dp_count = lax.axis_size("dp")
    query_count, pick_count = neg_blocks.shape
    embed_width = partial_sum.shape[2]
    row_count = query_count * pick_count
    capacity = max(2, -(-row_count // dp_count))
    slots_all = dp_count * capacity
    owners = neg_blocks.reshape(row_count)
    owner_hits = (owners[:, None] == jnp.arange(dp_count, dtype=jnp.int32)[None, :]).astype(
        jnp.int32
    )
    order = jnp.arange(row_count, dtype=jnp.int32)
    before = (order[None, :] < order[:, None]).astype(jnp.float32)
    earlier = jnp.dot(
        before, owner_hits.astype(jnp.float32), preferred_element_type=jnp.float32
    ).astype(jnp.int32)
    slot_rank = jnp.sum(earlier * owner_hits, axis=1)
    slot_ids = owners * capacity + slot_rank
    matches = (slot_ids[None, :] == jnp.arange(slots_all, dtype=jnp.int32)[:, None]).astype(
        jnp.int32
    )
    chosen = jnp.sum(matches.reshape(slots_all, query_count, pick_count), axis=2)
    token_share = lax.psum_scatter(partial_sum, "mp", scatter_dimension=1, tiled=True)
    share_vecs = unit_rows(token_share).astype(jnp.bfloat16)
    quarter = share_vecs.shape[1]
    token_part = jnp.einsum(
        "sq,qte->ste", chosen.astype(jnp.bfloat16), share_vecs, preferred_element_type=jnp.float32
    ).astype(jnp.bfloat16)
    token_part = token_part.reshape(dp_count, capacity, quarter, embed_width)
    arrived = lax.all_to_all(token_part, "dp", split_axis=0, concat_axis=0, tiled=True)
    joined = lax.all_gather(arrived, "mp", axis=2, tiled=True)
    tokens = joined.shape[2]
    scores = soft_scores(joined.reshape(slots_all, tokens, embed_width), passage_vecs).reshape(
        dp_count, capacity, -1
    )
    returned = lax.all_to_all(scores, "dp", split_axis=0, concat_axis=0, tiled=True)
    home_scores = returned.reshape(slots_all, -1)[slot_ids].reshape(query_count, pick_count, -1)
    teacher_logp = teacher - jnp.log(jnp.sum(jnp.exp(teacher), axis=(1, 2), keepdims=True))
    student = lax.all_gather(home_scores, "mp", axis=2, tiled=True)
    kl_loss = jnp.sum(jnp.exp(teacher_logp) * (teacher_logp - student), axis=(1, 2)) + jnp.log(
        jnp.sum(jnp.exp(student), axis=(1, 2))
    )
    return kl_loss


def solution(mesh):
    in_specs = (
        P("dp", None, "mp"),
        P("mp", None),
        P(("dp", "mp"), None, None),
        P("dp", None, None),
        P("dp", None),
    )
    out_specs = P("dp")
    dp, mp = mesh.shape["dp"], mesh.shape["mp"]

    def whole(query_hidden, query_proj, passages, teacher, neg_blocks):
        qd, picks = neg_blocks.shape[0] // dp, neg_blocks.shape[1]
        cap = max(2, -(-(qd * picks) // dp))
        share = query_hidden.shape[1] // mp
        own_p = passages.shape[0] // (dp * mp)
        fits = (
            mp == 4 and dp & (dp - 1) == 0 and dp * mp <= 64 and share % 8 == 0
            and cap % 16 == 0 and cap <= 256 and own_p % 8 == 0 and own_p <= 64
        )
        return jax.shard_map(
            fused_device if fits else per_device, mesh=mesh, in_specs=in_specs,
            out_specs=out_specs, check_vma=False,
        )(query_hidden, query_proj, passages, teacher, neg_blocks)

    return whole
```

time: 41.4 us -> 33.8 us (0.82)
  Pallas kernels: 36.6 us -> 32.6 us
  local copies, waits for them, and re-layouts: 4.17 us -> 1.1 us
    pallas_call x1, Pallas kernels: 36.6 us -> 32.6 us  [fused_device(): pl.pallas_call(functools.partial(fused_kernel, dp, mp, cap), out_shape=ja...]
    unnamed x11 -> x3, local copies, waits for them, and re-layouts: 3.91 us -> 1.1 us
where the time goes in v3:
time: 33.8 us; the launch traced here: 33.7 us
  Pallas kernels  32.6 us (96%)
  local copies, waits for them, and re-layouts  1.1 us (3%)
    pallas_call x1, Pallas kernels, fused_device(): pl.pallas_call(functools.partial(fused_kernel, dp, mp, cap), out_shape=ja...  32.6 us
    unnamed x3, local copies, waits for them, and re-layouts  1.1 us

profile of v3, /device:TPU:0, one launch (start us, length us, event | category | flops | bytes accessed | tf_op | source)
XLA Modules:
  0.0 33.7 jit_solution(8565845232810134928)
XLA Ops:
  0.0 32.6 %shard_map.55 = f32[1,32]{1,0:T(1,128)} custom-call(bf16[32,32,192]{2,1,0:T(8,128)(2,1)} %hid_hbm.1, bf16[192,128]{1,0:T(8,128)(2,1)} %proj_hbm.1, bf16[16,128,128]{2,1,0:T(8,128)(2,1)} %pas_hbm.1, f32[32,4,64]{2,1,0:T(4,128)} %teach_hbm.1, s32[4,32]{1,0:T(4,128)} %bitcast.2), custom_call_target="tpu_custom_call" | custom-call | tf_op jit(solution)/shard_map/pallas_call | solution.py:262
  32.6 0.0 copy-start
  32.6 0.6 %copy-done = f32[1,32]{1,0:T(1,128)S(1)} copy-done((f32[1,32]{1,0:T(1,128)S(1)}, f32[1,32]{1,0:T(1,128)}, u32[]{:S(2)}) %copy-start) | copy-done | bytes 152
  33.2 0.5 %copy.7 = f32[32]{0:T(128)} copy(f32[32]{0:T(128)S(1)} %bitcast.3) | data formatting | bytes 256
Async XLA Ops:
  32.6 0.6 %copy-start = (f32[1,32]{1,0:T(1,128)S(1)}, f32[1,32]{1,0:T(1,128)}, u32[]{:S(2)}) copy-start(f32[1,32]{1,0:T(1,128)} %shard_map.55) | copy-start | bytes 388

commit v4 on v3

--- a/solution.py
+++ b/solution.py
@@ -201,7 +201,7 @@
     remote(pvecs.at[1 - c], pvecs.at[1 - c], p_send, p_recv, d, sib).wait_recv()
     ahead = 1
     for j in range(dp):
-        while ahead < dp and ahead <= j + 2:
+        while ahead < dp and ahead <= j + 4:
             arrive(ahead)
             ahead = ahead + 1
         complete(j)

time: 33.8 us -> 33.1 us (0.979)
  Pallas kernels: 32.6 us -> 31.8 us
    pallas_call x1, Pallas kernels: 32.6 us -> 31.8 us  [fused_device(): pl.pallas_call(functools.partial(fused_kernel, dp, mp, cap), out_shape=ja...]
where the time goes in v4:
time: 33.1 us; the launch traced here: 32.9 us
  Pallas kernels  31.8 us (96%)
  local copies, waits for them, and re-layouts  1.1 us (3%)
    pallas_call x1, Pallas kernels, fused_device(): pl.pallas_call(functools.partial(fused_kernel, dp, mp, cap), out_shape=ja...  31.8 us
    unnamed x3, local copies, waits for them, and re-layouts  1.1 us

profile of v4, /device:TPU:0, one launch (start us, length us, event | category | flops | bytes accessed | tf_op | source)
XLA Modules:
  0.0 32.9 jit_solution(14683024921276189060)
XLA Ops:
  0.0 31.8 %shard_map.55 = f32[1,32]{1,0:T(1,128)} custom-call(bf16[32,32,192]{2,1,0:T(8,128)(2,1)} %hid_hbm.1, bf16[192,128]{1,0:T(8,128)(2,1)} %proj_hbm.1, bf16[16,128,128]{2,1,0:T(8,128)(2,1)} %pas_hbm.1, f32[32,4,64]{2,1,0:T(4,128)} %teach_hbm.1, s32[4,32]{1,0:T(4,128)} %bitcast.2), custom_call_target="tpu_custom_call" | custom-call | tf_op jit(solution)/shard_map/pallas_call | solution.py:262
  31.8 0.0 copy-start
  31.8 0.6 %copy-done = f32[1,32]{1,0:T(1,128)S(1)} copy-done((f32[1,32]{1,0:T(1,128)S(1)}, f32[1,32]{1,0:T(1,128)}, u32[]{:S(2)}) %copy-start) | copy-done | bytes 152
  32.4 0.5 %copy.7 = f32[32]{0:T(128)} copy(f32[32]{0:T(128)S(1)} %bitcast.3) | data formatting | bytes 256
Async XLA Ops:
  31.8 0.6 %copy-start = (f32[1,32]{1,0:T(1,128)S(1)}, f32[1,32]{1,0:T(1,128)}, u32[]{:S(2)}) copy-start(f32[1,32]{1,0:T(1,128)} %shard_map.55) | copy-start | bytes 388
